TPU v7x, 32 devices: a whole 2x2x4 slice. The times are simulated.
32 devices in a mesh: layer: 1, energy: 16 (over z, y, core), kpt: 2 (over x).
Axes of the slice: x: 2, y: 2, z: 4, core: 2. Of those that a mesh axis runs over, the one named last changes fastest.
Arguments:
- source: bfloat16 [1, 2, 8, 128, 4, 1024], P('layer', None, 'kpt', 'energy'), may hold values from -6 to 6
- basis: bfloat16 [1, 1024, 1024], P('layer'), may hold values from -0.1875 to 0.1875
- coupling: bfloat16 [1, 1024, 1024], P('layer'), may hold values from -0.25 to 0.25
- levels: float32 [1, 1024], P('layer'), may hold values from -2 to 2
- sigma_real: float32 [1, 128, 1024], P('layer', 'energy'), may hold values from -2.5 to 2.5
- broadening: float32 [1, 128, 1024], P('layer', 'energy'), may hold values from 0.05 to 1
- transverse: float32 [8], P('kpt'), may hold values from -1 to 1
- counts: int32 [1], P('layer'), may hold values from 512 to 1024
- occupation: float32 [128, 4], P('energy'), may hold values from 0.02 to 0.98
- kweight: int32 [8], replicated, may hold values from 1 to 4
- shifts: int32 [512], replicated, may hold values from 1 to 63
- emission: float32 [512], replicated, may hold values from 0.0009765625 to 0.0078125
- absorption: float32 [512], replicated, may hold values from 0.000390625 to 0.00390625
Outputs:
- sigma_lesser: float32 [1, 1024, 128], P('layer', 'energy')
- sigma_greater: float32 [1, 1024, 128], P('layer', 'energy')
All inputs are finite; a program needn't handle non-finite values.
Results may differ from a plain program's by a relative error of at most 0.0015.
Values may be sent and summed in bfloat16 or wider, within the bound.
No kernel may reach another device: no remote copies, remote signals or barrier semaphores. Data moves between devices by JAX's collectives and lax.ppermute only.
A program may use at most 64 MiB of HBM per device.

v0:
```python
import jax
import jax.numpy as jnp
from jax import lax
from jax.sharding import PartitionSpec as P

ETA = 1.0


def from_behind(shard, axis, by):
    size = lax.axis_size(axis)
    pairs = [(i, i + by) for i in range(size) if 0 <= i + by < size]
    return lax.ppermute(shard, axis, pairs)


def toeplitz(ahead, behind, count):
    period = jnp.concatenate([ahead, jnp.zeros((1,), jnp.float32), behind[1:][::-1]])
    tiled = jnp.tile(period, count)
    skewed = tiled[: count * (2 * count - 1)].reshape(count, 2 * count - 1)
    return skewed[:, :count]


def kernels(shifts, emission, absorption, count):
    grid = jnp.arange(count, dtype=jnp.int32)
    onehot = (shifts[:, None] == grid[None, :]).astype(jnp.float32)
    c_em = jnp.dot(emission, onehot, precision=lax.Precision.HIGHEST)
    c_ab = jnp.dot(absorption, onehot, precision=lax.Precision.HIGHEST)
    return (toeplitz(c_em, c_ab, count), toeplitz(c_ab, c_em, count))


def layer_map(prev, src, basis, coupling, g_real, g_imag):
    rows = prev.shape[1]
    width = prev.shape[2]
    x_val = jnp.dot(prev.reshape(2 * rows, width), coupling, preferred_element_type=jnp.float32)
    x_val = (x_val.reshape(2, rows, width) + src.astype(jnp.float32)).astype(jnp.bfloat16)
    y_val = jnp.dot(
        x_val.reshape(2 * rows, width), basis, preferred_element_type=jnp.float32
    ).reshape(2, rows, width)
    z_val = jnp.stack(
        [y_val[0] * g_real - y_val[1] * g_imag, y_val[0] * g_imag + y_val[1] * g_real]
    ).astype(jnp.bfloat16)
    psi = lax.dot_general(
        z_val.reshape(2 * rows, width),
        basis,
        (((1,), (1,)), ((), ())),
        preferred_element_type=jnp.float32,
    )
    return psi.reshape(2, rows, width).astype(jnp.bfloat16)


def on_device(
    source,
    basis,
    coupling,
    levels,
    sigma_real,
    broadening,
    transverse,
    counts,
    occupation,
    kweight,
    shifts,
    emission,
    absorption,
):
    kcount = source.shape[2]
    ecount = source.shape[3]
    modes = source.shape[4]
    width = source.shape[5]
    rows = kcount * ecount * modes
    energy_devs = lax.axis_size("energy")
    layer_devs = lax.axis_size("layer")
    all_energies = ecount * energy_devs
    layer_pos = lax.axis_index("layer")
    first_energy = lax.axis_index("energy") * ecount
    first_k = lax.axis_index("kpt") * kcount
    energy = (first_energy + jnp.arange(ecount, dtype=jnp.int32)).astype(jnp.float32)
    energy = (energy + 0.5) * (4.0 / all_energies) - 2.0
    real_part = (
        energy[None, :, None]
        - levels[0][None, None, :]
        - transverse[:, None, None]
        - sigma_real[0][None]
    )
    imag_part = ETA + broadening[0][None]
    denom = real_part * real_part + imag_part * imag_part
    active = (jnp.arange(width, dtype=jnp.int32) < counts[0]).astype(jnp.float32)
    g_real = active * real_part / denom
    g_imag = -active * imag_part / denom * jnp.ones_like(real_part)
    full_shape = (kcount, ecount, modes, width)
    g_real = jnp.broadcast_to(g_real[:, :, None, :], full_shape).reshape(rows, width)
    g_imag = jnp.broadcast_to(g_imag[:, :, None, :], full_shape).reshape(rows, width)
    src = source[0].reshape(2, rows, width)
    layer_basis = basis[0]
    layer_coupling = coupling[0]
    stored = jnp.zeros((2, rows, width), jnp.bfloat16)

    def sweep_all(step, state):
        carry, kept = state
        kept = lax.cond(
            step == layer_pos,
            lambda: layer_map(carry, src, layer_basis, layer_coupling, g_real, g_imag),
            lambda: kept,
        )
        carry = from_behind(kept, "layer", 1)
        return (carry, kept)

    carry_zero = jnp.zeros((2, rows, width), jnp.bfloat16)
    carry_end, psi = lax.fori_loop(0, layer_devs, sweep_all, (carry_zero, stored))
    weights = lax.dynamic_slice(kweight, (first_k,), (kcount,)).astype(jnp.float32)
    total = jnp.sum(kweight).astype(jnp.float32)
    values = psi.astype(jnp.float32)
    magnitude = (values[0] * values[0] + values[1] * values[1]).reshape(
        kcount, ecount, modes, width
    )
    per_mode = jnp.sum(magnitude * weights[:, None, None, None], axis=0)
    lesser = jnp.einsum("emo,em->eo", per_mode, occupation, precision=lax.Precision.HIGHEST) / total
    greater = (
        jnp.einsum("emo,em->eo", per_mode, 1.0 - occupation, precision=lax.Precision.HIGHEST)
        / total
    )
    dens = jnp.stack([lesser, greater])
    k_less, k_great = kernels(shifts, emission, absorption, all_energies)
    summed = lax.psum(dens, "kpt")
    mixed = lax.all_to_all(summed, "energy", split_axis=2, concat_axis=1, tiled=True)
    out_less = jnp.dot(k_less, mixed[0], precision=lax.Precision.HIGHEST).T[None]
    out_great = jnp.dot(k_great, mixed[1], precision=lax.Precision.HIGHEST).T[None]
    return (out_less, out_great)


def solution(mesh):
    in_specs = (
        P("layer", None, "kpt", "energy", None, None),
        P("layer", None, None),
        P("layer", None, None),
        P("layer", None),
        P("layer", "energy", None),
        P("layer", "energy", None),
        P("kpt"),
        P("layer"),
        P("energy", None),
        P(),
        P(),
        P(),
        P(),
    )
    out_specs = (P("layer", "energy", None), P("layer", "energy", None))
    return jax.shard_map(
        on_device, mesh=mesh, in_specs=in_specs, out_specs=out_specs, check_vma=False
    )
```

profile of v0, /device:TPU:0, one launch (start us, length us, event | category | flops | bytes accessed | tf_op | source)
XLA Modules:
  0.0 94.6 jit_solution(9937887486845216017)
XLA Ops:
  7.2 0.0 copy-start
  7.2 0.0 all-reduce.2.cloned.1.call-start
  8.1 0.8 multiply_bitcast_fusion
  8.8 0.8 broadcast_subtract_fusion
  9.6 0.9 fusion.27
  10.5 0.1 broadcast_in_dim.8
  10.6 0.2 reshape.115
  10.8 0.9 broadcast_in_dim.9
  11.7 1.2 %reshape.116 = f32[128,1024]{1,0:T(8,128)S(1)} reshape(f32[4,8,4,1024]{3,2,1,0:T(4,128)} %broadcast_in_dim.9) | data formatting | bytes 1048576 | tf_op jit(solution)/shard_map/reshape | solution.py:91
  12.9 2.1 %reshape.119 = f32[2,128,1024]{2,1,0:T(8,128)} reshape(bf16[1,2,4,8,4,1024]{5,4,3,2,1,0:T(4,128)(2,1)} %param.13) | data formatting | bytes 1572864 | tf_op jit(solution)/shard_map/while/body/eval_jaxpr/cond/branch_1_fun/convert_element_type | solution.py:34
  15.0 2.6 %fusion.15 = bf16[2,128,1024]{2,1,0:T(8,128)(2,1)S(1)} fusion(f32[2,128,1024]{2,1,0:T(8,128)} %reshape.119, bf16[1,1024,1024]{2,1,0:T(8,128)(2,1)} %param.15), kind=kOutput, calls=%fused_computation.9 | convolution fusion | flops 537395200 | bytes 3670016 | tf_op jit(solution)/shard_map/while/body/eval_jaxpr/cond/branch_1_fun/dot_general | solution.py:33
  17.6 0.0 copy-done
  17.6 0.7 fusion.2
  18.3 0.2 fusion.22
  18.6 0.7 fusion.12
  19.3 0.0 copy-start.5
  19.3 0.0 copy-start.1
  19.3 0.1 fusion.18
  19.4 0.0 copy-start.2
  19.4 0.0 copy-start.3
  19.4 0.0 copy-start.4
  19.4 0.1 add.84
  19.6 0.4 copy-done.5
  20.0 0.6 reduce_sum.19
  20.6 0.1 dynamic-slice_convert_fusion
  20.7 0.0 copy-done.1
  20.7 0.1 copy.27
  20.8 0.1 copy.25
  20.8 0.2 multiply_reduce_fusion
  21.0 0.3 fusion.44
  21.4 0.3 fusion.43
  22.4 1.3 %copy.21 = f32[2,8,1024]{1,0,2:T(2,128)} copy(f32[2,8,1024]{2,1,0:T(8,128)S(1)} %pad_maximum_fusion) | data formatting | bytes 131072 | tf_op jit(solution)/shard_map/stack | solution.py:121
  23.7 0.0 all-reduce.2.cloned.1.call-update
  23.7 0.0 copy-done.2
  23.7 0.0 copy-done.3
  23.7 0.3 convolution_bitcast_fusion.2
  24.0 0.1 slice.51
  24.1 0.1 rev.6
  24.2 0.0 copy-done.4
  24.2 0.3 convolution_bitcast_fusion.3
  24.5 0.1 slice.55
  24.6 0.1 rev.7
  24.7 0.1 fusion.38
  24.8 0.1 copy.31
  24.8 0.3 reshape.118
  25.2 41.4 %all-reduce.2.cloned.1.call-done = f32[2,8,1024]{1,0,2:T(2,128)} async-done(((f32[2,8,1024]{1,0,2:T(2,128)}), f32[2,8,1024]{1,0,2:T(2,128)}) %all-reduce.2.cloned.1.call-update) | async-done | bytes 65552 | tf_op jit(solution)/shard_map/psum | solution.py:123
  66.6 3.4 %reshape.130 = f32[16,1,1024]{2,1,0:T(1,128)} reshape(f32[1024,2,8]{2,1,0:T(2,128)} %bitcast.83) | data formatting | bytes 131072
  70.1 5.6 %all-to-all-start = ((f32[16,1,1024]{2,1,0:T(1,128)}), f32[16,1,1024]{2,1,0:T(1,128)S(1)}, u32[]{:S(2)}, u32[]{:S(2)}) async-start(f32[16,1,1024]{2,1,0:T(1,128)} %reshape.130), calls=%async_computation | async-start | bytes 131072 | tf_op jit(solution)/shard_map/all_to_all | solution.py:124
  75.7 0.1 copy.30
  75.8 0.3 reshape.117
  76.1 6.5 %all-to-all-done = f32[16,1,1024]{2,1,0:T(1,128)S(1)} async-done(((f32[16,1,1024]{2,1,0:T(1,128)}), f32[16,1,1024]{2,1,0:T(1,128)S(1)}, u32[]{:S(2)}, u32[]{:S(2)}) %all-to-all-start) | async-done | bytes 65568 | tf_op jit(solution)/shard_map/all_to_all | solution.py:124
  82.6 0.5 broadcast.114
  83.1 0.8 reduce
  83.9 1.6 %reshape.131 = f32[1024,2,8]{2,1,0:T(2,128)S(1)} reshape(f32[16,1024]{1,0:T(8,128)S(1)} %reduce) | data formatting | bytes 131072
  85.5 0.5 copy.29
  86.0 0.9 convolution_bitcast_fusion
  86.9 0.9 convolution_bitcast_fusion.1
  (9 shorter events, 0.1 us)
Async XLA Ops:
  7.2 10.4 %copy-start = (bf16[1,1024,1024]{2,1,0:T(8,128)(2,1)S(1)}, bf16[1,1024,1024]{2,1,0:T(8,128)(2,1)}, u32[]{:S(2)}) copy-start(bf16[1,1024,1024]{2,1,0:T(8,128)(2,1)} %param.14) | copy-start | bytes 6291460
  7.2 59.4 %all-reduce.2.cloned.1.call-start = ((), (), s32[]{:S(2)}) async-start(), calls=%async_computation.1 | async-start | bytes 2097152 | tf_op jit(solution)/shard_map/psum | solution.py:123
  19.3 0.7 copy-start.5
  19.3 1.4 %copy-start.1 = (f32[8,4]{0,1:T(4,128)S(1)}, f32[8,4]{0,1:T(4,128)}, u32[]{:S(2)}) copy-start(f32[8,4]{0,1:T(4,128)} %param.21) | copy-start | bytes 388
  19.4 4.3 %copy-start.2 = (f32[512]{0:T(512)S(1)}, f32[512]{0:T(512)}, u32[]{:S(2)}) copy-start(f32[512]{0:T(512)} %param.25) | copy-start | bytes 6148
  19.4 4.3 %copy-start.3 = (s32[512]{0:T(512)S(1)}, s32[512]{0:T(512)}, u32[]{:S(2)}) copy-start(s32[512]{0:T(512)} %param.23) | copy-start | bytes 6148
  19.4 4.8 %copy-start.4 = (f32[512]{0:T(512)S(1)}, f32[512]{0:T(512)}, u32[]{:S(2)}) copy-start(f32[512]{0:T(512)} %param.24) | copy-start | bytes 6148
  70.1 12.5 %all-to-all-start = ((f32[16,1,1024]{2,1,0:T(1,128)}), f32[16,1,1024]{2,1,0:T(1,128)S(1)}, u32[]{:S(2)}, u32[]{:S(2)}) async-start(f32[16,1,1024]{2,1,0:T(1,128)} %reshape.130), calls=%async_computation | async-start | bytes 131072 | tf_op jit(solution)/shard_map/all_to_all | solution.py:124
Sparse Core Ops, SparseCore 0:
  23.8 42.7 all-reduce.1
where the time goes:
time: 95.1 us; the launch traced here: 94.6 us
  waiting for transfers between devices  47.9 us (50%)
  between operations  15.8 us (17%)
  local copies, waits for them, and re-layouts  13.7 us (14%)
  matrix products  7.05 us (7%)
  starting transfers between devices  5.66 us (6%)
  other arithmetic  4.51 us (5%)
    psum x1, waiting for transfers between devices, on_device(): summed = lax.psum(dens, 'kpt')  41.4 us
    all_to_all x1, waiting for transfers between devices, on_device(): lax.all_to_all(summed, 'energy', split_axis=2, concat_axis=1, tiled=True)  6.46 us
    unnamed x19, local copies, waits for them, and re-layouts  5.68 us
    all_to_all x1, starting transfers between devices, on_device(): lax.all_to_all(summed, 'energy', split_axis=2, concat_axis=1, tiled=True)  5.62 us
    dot_general x1, matrix products, layer_map(): jnp.dot(prev.reshape(2 * rows, width), coupling, preferred_element_type=j...  2.56 us
    convert_element_type x1, local copies, waits for them, and re-layouts, layer_map(): src.astype(jnp.float32)  2.09 us
  transfers between devices with their start and end apart: 2, of which 2 were waited for; matrix products, arithmetic and copies ran while one was open for 2% of the time, Pallas kernels for 0%

commit v1 on v0

v1 whole, which is shorter than its diff:
```python
import functools

import jax
import jax.numpy as jnp
from jax import lax
from jax.experimental import pallas as pl
from jax.experimental.pallas import tpu as pltpu
from jax.sharding import PartitionSpec as P

ETA = 1.0
F32 = jnp.float32
BF16 = jnp.bfloat16
VMEM = pltpu.VMEM
SMEM = pltpu.SMEM


def from_behind(shard, axis, by):
    size = lax.axis_size(axis)
    pairs = [(i, i + by) for i in range(size) if 0 <= i + by < size]
    return lax.ppermute(shard, axis, pairs)


def chunk_of(width):
    return 256 if width % 256 == 0 else width


def in_three(value):
    high = value.astype(BF16)
    rest = value - high.astype(F32)
    middle = rest.astype(BF16)
    low = (rest - middle.astype(F32)).astype(BF16)
    return high, middle, low


def write_toeplitz(shifts_ref, emission_ref, absorption_ref, mix_ref):
    count = mix_ref.shape[0]
    points = shifts_ref.shape[1]
    spot = lax.broadcasted_iota(jnp.int32, (2 * count, points), 0)
    shift = shifts_ref[...]
    hit = jnp.where(spot < count, spot, 2 * count - spot) == shift
    onehot = jnp.where(hit, 1.0, 0.0).astype(BF16)
    pieces = in_three(emission_ref[...]) + in_three(absorption_ref[...])
    rows = jnp.concatenate([p.astype(F32) for p in pieces] + [jnp.zeros((2, points), F32)], axis=0)
    sums = lax.dot_general(
        rows.astype(BF16), onehot, (((1,), (1,)), ((), ())), preferred_element_type=F32
    )
    emit = sums[0:1] + sums[1:2] + sums[2:3]
    absorb = sums[3:4] + sums[4:5] + sums[5:6]
    lane = lax.broadcasted_iota(jnp.int32, (1, 2 * count), 1)
    for which, period in enumerate(
        (jnp.where(lane < count, absorb, emit), jnp.where(lane < count, emit, absorb))
    ):
        square = jnp.broadcast_to(period, (count, 2 * count))
        skewed = pltpu.roll(square, 0, 1, stride=1, stride_axis=0)
        mix_ref[:, which * count : (which + 1) * count] = skewed[:, :count]


def strided(ref, tiles, first, count, step):
    return jnp.concatenate([ref[t, pl.ds(first, count, stride=step), :] for t in tiles], axis=1)


def layer_kernel(
    has_prev,
    count_ref,
    trans_hbm,
    kweight_hbm,
    shifts_hbm,
    emission_hbm,
    absorption_hbm,
    levels_hbm,
    sigma_hbm,
    broad_hbm,
    occ_hbm,
    src_hbm,
    basis_hbm,
    *rest,
):
    if has_prev:
        prev_hbm, coupling_hbm, send_ref, mix_ref, psi_ref, *rest, prev_ref, coupling_ref = rest
    else:
        send_ref, mix_ref, *rest = rest
    (
        trans_ref,
        kweight_ref,
        shifts_ref,
        emission_ref,
        absorption_ref,
        levels_ref,
        sigma_ref,
        broad_ref,
        occ_ref,
        src_ref,
        basis_ref,
        g_ref,
        y_ref,
        z_ref,
        sems,
    ) = rest
    kcount, ecount, modes, width = src_ref.shape[2:]
    rows = kcount * ecount * modes
    chunk = chunk_of(width)
    parts = width // chunk
    lanes = y_ref.shape[2]

    pairs = [
        (shifts_hbm, shifts_ref),
        (emission_hbm, emission_ref),
        (absorption_hbm, absorption_ref),
        (trans_hbm, trans_ref),
        (kweight_hbm, kweight_ref),
        (levels_hbm, levels_ref),
        (sigma_hbm, sigma_ref),
        (broad_hbm, broad_ref),
        (occ_hbm, occ_ref),
        (src_hbm, src_ref),
    ]
    for part in range(parts):
        cols = pl.ds(part * chunk, chunk)
        pairs.append((basis_hbm.at[0, :, cols], basis_ref.at[:, cols]))
    if has_prev:
        pairs += [(prev_hbm, prev_ref), (coupling_hbm, coupling_ref)]
    copies = [pltpu.make_async_copy(a, b, sems.at[i]) for i, (a, b) in enumerate(pairs)]
    for copy in copies:
        copy.start()
    for copy in copies[:3]:
        copy.wait()
    write_toeplitz(shifts_ref, emission_ref, absorption_ref, mix_ref)

    for copy in copies[3:9]:
        copy.wait()
    first_energy = lax.axis_index("energy") * ecount
    first_k = lax.axis_index("kpt") * kcount
    energy = (first_energy + lax.broadcasted_iota(jnp.int32, (ecount, 1), 0)).astype(F32)
    energy = (energy + 0.5) * (4.0 / mix_ref.shape[0]) - 2.0
    mode = lax.broadcasted_iota(jnp.int32, (1, width), 1)
    active = jnp.where(mode < count_ref[0], 1.0, 0.0)
    base = energy - levels_ref[...] - sigma_ref[0]
    imag = ETA + broad_ref[0]
    imag2 = imag * imag
    for k in range(kcount):
        real = base - trans_ref[k]
        scale = active / (real * real + imag2)
        g_ref[0, k] = real * scale
        g_ref[1, k] = -imag * scale

    copies[9].wait()
    x_val = src_ref[0].reshape(2 * rows, width)
    if has_prev:
        copies[10 + parts].wait()
        copies[11 + parts].wait()
        carried = jnp.dot(
            prev_ref[...], coupling_ref[0], preferred_element_type=F32
        )
        x_val = (carried + x_val.astype(F32)).astype(BF16)
    for part in range(parts):
        cols = pl.ds(part * chunk, chunk)
        copies[10 + part].wait()
        y_val = jnp.dot(x_val, basis_ref[:, cols], preferred_element_type=F32)
        for t in range(chunk // lanes):
            y_ref[part * (chunk // lanes) + t] = y_val[:, t * lanes : (t + 1) * lanes]
        tiles = range(part * (chunk // lanes), (part + 1) * (chunk // lanes))
        for k in range(kcount):
            g_real = g_ref[0, k, :, cols]
            g_imag = g_ref[1, k, :, cols]
            z_re = []
            z_im = []
            for m in range(modes):
                first = k * ecount * modes + m
                y_re = strided(y_ref, tiles, first, ecount, modes)
                y_im = strided(y_ref, tiles, rows + first, ecount, modes)
                z_re.append(y_re * g_real - y_im * g_imag)
                z_im.append(y_re * g_imag + y_im * g_real)
            group = pl.ds(k * ecount * modes, ecount * modes)
            z_ref[group, cols] = jnp.concatenate(z_re, axis=0).astype(BF16)
            group = pl.ds(rows + k * ecount * modes, ecount * modes)
            z_ref[group, cols] = jnp.concatenate(z_im, axis=0).astype(BF16)

    total = kweight_ref[0]
    for k in range(1, kweight_ref.shape[0]):
        total = total + kweight_ref[k]
    total = jnp.full((ecount, 1), total, jnp.int32).astype(F32)
    weights = [kweight_ref[first_k + k].astype(F32) for k in range(kcount)]
    diagonal = lax.broadcasted_iota(jnp.int32, (ecount, ecount), 0) == lax.broadcasted_iota(
        jnp.int32, (ecount, ecount), 1
    )
    filled = []
    for m in range(modes):
        row = jnp.broadcast_to(occ_ref[m : m + 1, :], (ecount, ecount))
        filled.append(jnp.sum(jnp.where(diagonal, row, 0.0), axis=1, keepdims=True))
    less_of = [f / total for f in filled]
    great_of = [(1.0 - f) / total for f in filled]

    targets = send_ref.shape[0]
    copies_k = send_ref.shape[1]
    block = width // targets
    for part in range(parts):
        psi = lax.dot_general(
            z_ref[...],
            basis_ref[pl.ds(part * chunk, chunk), :],
            (((1,), (1,)), ((), ())),
            preferred_element_type=F32,
        )
        if has_prev:
            psi_ref[:, pl.ds(part * chunk, chunk)] = psi.astype(BF16)
        less = None
        great = None
        for m in range(modes):
            per_mode = None
            for k in range(kcount):
                first = (k * modes + m) * ecount
                re = psi[first : first + ecount]
                im = psi[rows + first : rows + first + ecount]
                term = (re * re + im * im) * weights[k]
                per_mode = term if per_mode is None else per_mode + term
            less = per_mode * less_of[m] if less is None else less + per_mode * less_of[m]
            great = per_mode * great_of[m] if great is None else great + per_mode * great_of[m]
        for t in range(chunk // block):
            both = jnp.concatenate(
                [less[:, t * block : (t + 1) * block], great[:, t * block : (t + 1) * block]], axis=1
            ).astype(BF16)
            for c in range(copies_k):
                send_ref[part * (chunk // block) + t, c] = both


def mix_kernel(got_ref, mix_ref, less_ref, great_ref):
    count = mix_ref.shape[0]
    got = got_ref[...].astype(F32)
    dens = jnp.sum(got, axis=1).reshape(count, got.shape[3])
    out = lax.dot_general(
        dens,
        mix_ref[...],
        (((0,), (0,)), ((), ())),
        precision=lax.Precision.HIGHEST,
        preferred_element_type=F32,
    )
    block = less_ref.shape[1]
    less_ref[0] = out[:block, :count]
    great_ref[0] = out[block:, count:]


def on_device(
    source,
    basis,
    coupling,
    levels,
    sigma_real,
    broadening,
    transverse,
    counts,
    occupation,
    kweight,
    shifts,
    emission,
    absorption,
):
    kcount, ecount, modes, width = source.shape[2:]
    rows = kcount * ecount * modes
    energy_devs = lax.axis_size("energy")
    k_devs = lax.axis_size("kpt")
    layer_devs = lax.axis_size("layer")
    all_energies = ecount * energy_devs
    block = width // energy_devs
    parts = width // chunk_of(width)
    vmem = pl.BlockSpec(memory_space=VMEM)
    hbm = pl.BlockSpec(memory_space=pltpu.HBM)
    operands = (
        counts,
        transverse,
        kweight,
        shifts[None],
        emission[None],
        absorption[None],
        levels,
        sigma_real,
        broadening,
        occupation.T,
        source,
        basis,
    )
    send_shape = jax.ShapeDtypeStruct((energy_devs, k_devs, ecount, 2 * block), BF16)
    mix_shape = jax.ShapeDtypeStruct((all_energies, 2 * all_energies), F32)
    scratch = (
        [SMEM(a.shape, a.dtype) for a in operands[1:3]]
        + [VMEM(a.shape, a.dtype) for a in operands[3:11]]
        + [
            VMEM((width, width), BF16),
            VMEM((2, kcount, ecount, width), F32),
            VMEM((width // 128, 2 * rows, 128), F32),
            VMEM((2 * rows, width), BF16),
        ]
    )
    psi_shape = jax.ShapeDtypeStruct((2 * rows, width), BF16)

    def layer(prev):
        has_prev = prev is not None
        more = (prev, coupling) if has_prev else ()
        in_hbm = [pltpu.with_memory_space_constraint(a, pltpu.HBM) for a in operands[1:] + more]
        sems = pltpu.SemaphoreType.DMA((10 + parts + len(more),))
        return pl.pallas_call(
            functools.partial(layer_kernel, has_prev),
            out_shape=(send_shape, mix_shape) + ((psi_shape,) if has_prev else ()),
            in_specs=[pl.BlockSpec(memory_space=SMEM)] + [hbm] * len(in_hbm),
            out_specs=(vmem,) * (3 if has_prev else 2),
            scratch_shapes=scratch + [sems] + [VMEM(a.shape, a.dtype) for a in more],
            compiler_params=pltpu.CompilerParams(vmem_limit_bytes=24 * 1024 * 1024),
        )(operands[0], *in_hbm)

    if layer_devs == 1:
        send, mix = layer(None)
    else:
        layer_pos = lax.axis_index("layer")

        def sweep(step, state):
            carry, kept = state
            kept = lax.cond(step == layer_pos, lambda: tuple(layer(carry)), lambda: kept)
            carry = kept[2].reshape(2, kcount, modes, ecount, width).transpose(0, 1, 3, 2, 4)
            carry = from_behind(carry.reshape(2 * rows, width), "layer", 1)
            return carry, kept

        stored = tuple(jnp.zeros(a.shape, a.dtype) for a in (send_shape, mix_shape, psi_shape))
        send, mix, _ = lax.fori_loop(0, layer_devs, sweep, (stored[2], stored))[1]
    got = lax.all_to_all(
        send.reshape(energy_devs * k_devs, ecount, 2 * block), ("energy", "kpt"), 0, 0, tiled=True
    ).reshape(energy_devs, k_devs, ecount, 2 * block)
    out_shape = jax.ShapeDtypeStruct((1, block, all_energies), F32)
    return pl.pallas_call(
        mix_kernel,
        out_shape=(out_shape, out_shape),
        in_specs=[vmem, vmem],
        out_specs=(vmem, vmem),
        compiler_params=pltpu.CompilerParams(vmem_limit_bytes=8 * 1024 * 1024),
    )(got, mix)


def solution(mesh):
    in_specs = (
        P("layer", None, "kpt", "energy", None, None),
        P("layer", None, None),
        P("layer", None, None),
        P("layer", None),
        P("layer", "energy", None),
        P("layer", "energy", None),
        P("kpt"),
        P("layer"),
        P("energy", None),
        P(),
        P(),
        P(),
        P(),
    )
    out_specs = (P("layer", "energy", None), P("layer", "energy", None))
    return jax.shard_map(
        on_device, mesh=mesh, in_specs=in_specs, out_specs=out_specs, check_vma=False
    )
```

time: 95.1 us -> 20.9 us (0.22)
  waiting for transfers between devices: 47.9 us -> 0 us
  blocking collectives: 0 us -> 14.7 us
  between operations: 15.8 us -> 1.29 us
  local copies, waits for them, and re-layouts: 13.7 us -> 0 us
  matrix products: 7.05 us -> 0 us
  starting transfers between devices: 5.66 us -> 0 us
  Pallas kernels: 0 us -> 4.76 us
  other arithmetic: 4.51 us -> 0 us
    psum x1 -> x0, waiting for transfers between devices: 41.4 us -> none  [on_device(): summed = lax.psum(dens, 'kpt')]
    all_to_all x0 -> x1, blocking collectives: none -> 14.7 us  [on_device(): lax.all_to_all(send.reshape(energy_devs * k_devs, ecount, 2 * block), ('e...]
    dot_general x9 -> x0, matrix products: 7.05 us -> none  [the longest x1 2.56 us: layer_map(): jnp.dot(prev.reshape(2 * rows, width), coupling, preferred_element_type=j...]
    all_to_all x1 -> x0, waiting for transfers between devices: 6.46 us -> none  [on_device(): lax.all_to_all(summed, 'energy', split_axis=2, concat_axis=1, tiled=True)]
    unnamed x19 -> x0, local copies, waits for them, and re-layouts: 5.68 us -> none
    all_to_all x1 -> x0, starting transfers between devices: 5.62 us -> none  [on_device(): lax.all_to_all(summed, 'energy', split_axis=2, concat_axis=1, tiled=True)]
    pallas_call x0 -> x2, Pallas kernels: none -> 4.76 us  [the longest x1 3.82 us: layer(): pl.pallas_call(functools.partial(layer_kernel, has_prev), out_shape=(send...]
    convert_element_type x1 -> x0, local copies, waits for them, and re-layouts: 2.09 us -> none  [layer_map(): src.astype(jnp.float32)]
  transfers between devices with their start and end apart: 2 -> 0, of which waited for: 2 -> 0; matrix products, arithmetic and copies ran while one was open for 2% -> 0% of each run, Pallas kernels for 0% -> 0%
where the time goes in v1:
time: 20.9 us; the launch traced here: 20.8 us
  blocking collectives  14.7 us (70%)
  Pallas kernels  4.76 us (23%)
  between operations  1.29 us (6%)
    all_to_all x1, blocking collectives, on_device(): lax.all_to_all(send.reshape(energy_devs * k_devs, ecount, 2 * block), ('e...  14.7 us
    pallas_call x1, Pallas kernels, layer(): pl.pallas_call(functools.partial(layer_kernel, has_prev), out_shape=(send...  3.82 us
    pallas_call x1, Pallas kernels, on_device(): pl.pallas_call(mix_kernel, out_shape=(out_shape, out_shape), in_specs=[vm...  0.93 us

profile of v1, /device:TPU:0, one launch (start us, length us, event | category | flops | bytes accessed | tf_op | source)
XLA Modules:
  0.0 20.8 jit_solution(13442332401196063778)
XLA Ops:
  1.3 3.8 %shard_map.131 = (bf16[16,2,8,128]{3,2,1,0:T(8,128)(2,1)S(1)}, f32[128,256]{1,0:T(8,128)S(1)}) custom-call(s32[1]{0:T(128)S(6)} %copy.14.count_ref, f32[4]{0:T(128)} %trans_hbm.1, s32[8]{0:T(128)} %kweight_hbm.1, s32[1,512]{1,0:T(1,128)} %bitcast.8, f32[1,512]{1,0:T(1,128)} %bitcast.9, f32[1,512]{1,0:T(1,128)} %bitcast.10, f32[1,1024]{1,0:T(1,128)} %levels_hbm.1, ...), custom_call_target="tpu_custom_call" | custom-call | tf_op jit(solution)/shard_map/pallas_call | solution.py:299
  5.1 14.7 %all_to_all.5 = bf16[32,8,128]{2,1,0:T(8,128)(2,1)S(1)} all-to-all(bf16[32,8,128]{2,1,0:T(8,128)(2,1)S(1)} %bitcast.7), channel_id=1, replica_groups=mesh['layer'=1,'energy'=16,'kpt'=2] {'energy','kpt'}, dimensions={0} | all-to-all | bytes 131072 | tf_op jit(solution)/shard_map/all_to_all | solution.py:322
  19.8 0.9 %shard_map.132 = (f32[1,64,128]{2,1,0:T(8,128)}, f32[1,64,128]{2,1,0:T(8,128)}) custom-call(bf16[16,2,8,128]{3,2,1,0:T(8,128)(2,1)S(1)} %bitcast.6, f32[128,256]{1,0:T(8,128)S(1)} %get-tuple-element.5.mix_ref), custom_call_target="tpu_custom_call" | custom-call | tf_op jit(solution)/shard_map/pallas_call | solution.py:326

commit v2 on v1

--- a/solution.py
+++ b/solution.py
@@ -94,6 +94,7 @@
         g_ref,
         y_ref,
         z_ref,
+        x_ref,
         sems,
     ) = rest
     kcount, ecount, modes, width = src_ref.shape[2:]
@@ -116,17 +117,14 @@
     ]
     for part in range(parts):
         cols = pl.ds(part * chunk, chunk)
-        pairs.append((basis_hbm.at[0, :, cols], basis_ref.at[:, cols]))
+        pairs.append((basis_hbm.at[0, cols, :], basis_ref.at[cols, :]))
     if has_prev:
         pairs += [(prev_hbm, prev_ref), (coupling_hbm, coupling_ref)]
     copies = [pltpu.make_async_copy(a, b, sems.at[i]) for i, (a, b) in enumerate(pairs)]
-    for copy in copies:
+    small, carried, wide = copies[:9], copies[10 + parts :], copies[9 : 10 + parts]
+    for copy in small + wide + carried:
         copy.start()
-    for copy in copies[:3]:
-        copy.wait()
-    write_toeplitz(shifts_ref, emission_ref, absorption_ref, mix_ref)
-
-    for copy in copies[3:9]:
+    for copy in small:
         copy.wait()
     first_energy = lax.axis_index("energy") * ecount
     first_k = lax.axis_index("kpt") * kcount
@@ -142,22 +140,25 @@
         scale = active / (real * real + imag2)
         g_ref[0, k] = real * scale
         g_ref[1, k] = -imag * scale
-
-    copies[9].wait()
-    x_val = src_ref[0].reshape(2 * rows, width)
-    if has_prev:
-        copies[10 + parts].wait()
-        copies[11 + parts].wait()
-        carried = jnp.dot(
-            prev_ref[...], coupling_ref[0], preferred_element_type=F32
-        )
-        x_val = (carried + x_val.astype(F32)).astype(BF16)
-    for part in range(parts):
+    write_toeplitz(shifts_ref, emission_ref, absorption_ref, mix_ref)
+
+    total = kweight_ref[0]
+    for k in range(1, kweight_ref.shape[0]):
+        total = total + kweight_ref[k]
+    total = jnp.full((ecount, 1), total, jnp.int32).astype(F32)
+    weights = [kweight_ref[first_k + k].astype(F32) for k in range(kcount)]
+    diagonal = lax.broadcasted_iota(jnp.int32, (ecount, ecount), 0) == lax.broadcasted_iota(
+        jnp.int32, (ecount, ecount), 1
+    )
+    filled = []
+    for m in range(modes):
+        row = jnp.broadcast_to(occ_ref[m : m + 1, :], (ecount, ecount))
+        filled.append(jnp.sum(jnp.where(diagonal, row, 0.0), axis=1, keepdims=True))
+    less_of = [f / total for f in filled]
+    great_of = [(1.0 - f) / total for f in filled]
+
+    def scale_modes(part):
         cols = pl.ds(part * chunk, chunk)
-        copies[10 + part].wait()
-        y_val = jnp.dot(x_val, basis_ref[:, cols], preferred_element_type=F32)
-        for t in range(chunk // lanes):
-            y_ref[part * (chunk // lanes) + t] = y_val[:, t * lanes : (t + 1) * lanes]
         tiles = range(part * (chunk // lanes), (part + 1) * (chunk // lanes))
         for k in range(kcount):
             g_real = g_ref[0, k, :, cols]
@@ -175,31 +176,10 @@
             group = pl.ds(rows + k * ecount * modes, ecount * modes)
             z_ref[group, cols] = jnp.concatenate(z_im, axis=0).astype(BF16)
 
-    total = kweight_ref[0]
-    for k in range(1, kweight_ref.shape[0]):
-        total = total + kweight_ref[k]
-    total = jnp.full((ecount, 1), total, jnp.int32).astype(F32)
-    weights = [kweight_ref[first_k + k].astype(F32) for k in range(kcount)]
-    diagonal = lax.broadcasted_iota(jnp.int32, (ecount, ecount), 0) == lax.broadcasted_iota(
-        jnp.int32, (ecount, ecount), 1
-    )
-    filled = []
-    for m in range(modes):
-        row = jnp.broadcast_to(occ_ref[m : m + 1, :], (ecount, ecount))
-        filled.append(jnp.sum(jnp.where(diagonal, row, 0.0), axis=1, keepdims=True))
-    less_of = [f / total for f in filled]
-    great_of = [(1.0 - f) / total for f in filled]
-
-    targets = send_ref.shape[0]
     copies_k = send_ref.shape[1]
-    block = width // targets
-    for part in range(parts):
-        psi = lax.dot_general(
-            z_ref[...],
-            basis_ref[pl.ds(part * chunk, chunk), :],
-            (((1,), (1,)), ((), ())),
-            preferred_element_type=F32,
-        )
+    block = width // send_ref.shape[0]
+
+    def densities(part, psi):
         if has_prev:
             psi_ref[:, pl.ds(part * chunk, chunk)] = psi.astype(BF16)
         less = None
@@ -220,6 +200,38 @@
             ).astype(BF16)
             for c in range(copies_k):
                 send_ref[part * (chunk // block) + t, c] = both
+
+    wide[0].wait()
+    x_ref[...] = src_ref[0].reshape(2 * rows, width)
+    if has_prev:
+        for copy in carried:
+            copy.wait()
+        brought = jnp.dot(prev_ref[...], coupling_ref[0], preferred_element_type=F32)
+        x_ref[...] = (brought + x_ref[...].astype(F32)).astype(BF16)
+    stages = min(2, parts)
+    for stage in range(stages):
+        first_part = stage * parts // stages
+        last_part = (stage + 1) * parts // stages
+        for part in range(first_part, last_part):
+            wide[1 + part].wait()
+        depth = pl.ds(first_part * chunk, (last_part - first_part) * chunk)
+        for part in range(parts):
+            cols = pl.ds(part * chunk, chunk)
+            y_val = jnp.dot(x_ref[:, depth], basis_ref[depth, cols], preferred_element_type=F32)
+            for t in range(chunk // lanes):
+                tile = part * (chunk // lanes) + t
+                piece = y_val[:, t * lanes : (t + 1) * lanes]
+                y_ref[tile] = piece if stage == 0 else y_ref[tile] + piece
+    for part in range(parts):
+        scale_modes(part)
+    for part in range(parts):
+        psi = lax.dot_general(
+            z_ref[...],
+            basis_ref[pl.ds(part * chunk, chunk), :],
+            (((1,), (1,)), ((), ())),
+            preferred_element_type=F32,
+        )
+        densities(part, psi)
 
 
 def mix_kernel(got_ref, mix_ref, less_ref, great_ref):
@@ -287,6 +299,7 @@
             VMEM((2, kcount, ecount, width), F32),
             VMEM((width // 128, 2 * rows, 128), F32),
             VMEM((2 * rows, width), BF16),
+            VMEM((2 * rows, width), BF16),
         ]
     )
     psi_shape = jax.ShapeDtypeStruct((2 * rows, width), BF16)

time: 20.9 us -> 20.2 us (0.967)
  Pallas kernels: 4.76 us -> 4.02 us
    pallas_call x1, Pallas kernels: 3.82 us -> 3.09 us  [layer(): pl.pallas_call(functools.partial(layer_kernel, has_prev), out_shape=(send...]
where the time goes in v2:
time: 20.2 us; the launch traced here: 20 us
  blocking collectives  14.7 us (73%)
  Pallas kernels  4.02 us (20%)
  between operations  1.29 us (6%)
    all_to_all x1, blocking collectives, on_device(): lax.all_to_all(send.reshape(energy_devs * k_devs, ecount, 2 * block), ('e...  14.7 us
    pallas_call x1, Pallas kernels, layer(): pl.pallas_call(functools.partial(layer_kernel, has_prev), out_shape=(send...  3.09 us
    pallas_call x1, Pallas kernels, on_device(): pl.pallas_call(mix_kernel, out_shape=(out_shape, out_shape), in_specs=[vm...  0.93 us

profile of v2, /device:TPU:0, one launch (start us, length us, event | category | flops | bytes accessed | tf_op | source)
XLA Modules:
  0.0 20.0 jit_solution(12033779158758831260)
XLA Ops:
  1.3 3.1 %shard_map.131 = (bf16[16,2,8,128]{3,2,1,0:T(8,128)(2,1)S(1)}, f32[128,256]{1,0:T(8,128)S(1)}) custom-call(s32[1]{0:T(128)S(6)} %copy.14.count_ref, f32[4]{0:T(128)} %trans_hbm.1, s32[8]{0:T(128)} %kweight_hbm.1, s32[1,512]{1,0:T(1,128)} %bitcast.8, f32[1,512]{1,0:T(1,128)} %bitcast.9, f32[1,512]{1,0:T(1,128)} %bitcast.10, f32[1,1024]{1,0:T(1,128)} %levels_hbm.1, ...), custom_call_target="tpu_custom_call" | custom-call | tf_op jit(solution)/shard_map/pallas_call | solution.py:312
  4.4 14.7 %all_to_all.5 = bf16[32,8,128]{2,1,0:T(8,128)(2,1)S(1)} all-to-all(bf16[32,8,128]{2,1,0:T(8,128)(2,1)S(1)} %bitcast.7), channel_id=1, replica_groups=mesh['layer'=1,'energy'=16,'kpt'=2] {'energy','kpt'}, dimensions={0} | all-to-all | bytes 131072 | tf_op jit(solution)/shard_map/all_to_all | solution.py:335
  19.1 0.9 %shard_map.132 = (f32[1,64,128]{2,1,0:T(8,128)}, f32[1,64,128]{2,1,0:T(8,128)}) custom-call(bf16[16,2,8,128]{3,2,1,0:T(8,128)(2,1)S(1)} %bitcast.6, f32[128,256]{1,0:T(8,128)S(1)} %get-tuple-element.5.mix_ref), custom_call_target="tpu_custom_call" | custom-call | tf_op jit(solution)/shard_map/pallas_call | solution.py:339

commit v3 on v2

--- a/solution.py
+++ b/solution.py
@@ -32,8 +32,8 @@
     return high, middle, low
 
 
-def write_toeplitz(shifts_ref, emission_ref, absorption_ref, mix_ref):
-    count = mix_ref.shape[0]
+def write_toeplitz(shifts_ref, emission_ref, absorption_ref, mix_ref, energy_devs, k_devs):
+    count = mix_ref.shape[1] // 4
     points = shifts_ref.shape[1]
     spot = lax.broadcasted_iota(jnp.int32, (2 * count, points), 0)
     shift = shifts_ref[...]
@@ -51,8 +51,15 @@
         (jnp.where(lane < count, absorb, emit), jnp.where(lane < count, emit, absorb))
     ):
         square = jnp.broadcast_to(period, (count, 2 * count))
-        skewed = pltpu.roll(square, 0, 1, stride=1, stride_axis=0)
-        mix_ref[:, which * count : (which + 1) * count] = skewed[:, :count]
+        skewed = pltpu.roll(square, 0, 1, stride=1, stride_axis=0)[:, :count]
+        high = skewed.astype(BF16).astype(F32)
+        for side, piece in enumerate((high, skewed - high)):
+            blocks = piece.reshape(energy_devs, 1, count // energy_devs, count)
+            blocks = jnp.broadcast_to(
+                blocks, (energy_devs, k_devs, count // energy_devs, count)
+            ).reshape(k_devs * count, count)
+            first = (2 * side + which) * count
+            mix_ref[:, first : first + count] = blocks.astype(BF16)
 
 
 def strided(ref, tiles, first, count, step):
@@ -129,7 +136,7 @@
     first_energy = lax.axis_index("energy") * ecount
     first_k = lax.axis_index("kpt") * kcount
     energy = (first_energy + lax.broadcasted_iota(jnp.int32, (ecount, 1), 0)).astype(F32)
-    energy = (energy + 0.5) * (4.0 / mix_ref.shape[0]) - 2.0
+    energy = (energy + 0.5) * (4.0 / (mix_ref.shape[1] // 4)) - 2.0
     mode = lax.broadcasted_iota(jnp.int32, (1, width), 1)
     active = jnp.where(mode < count_ref[0], 1.0, 0.0)
     base = energy - levels_ref[...] - sigma_ref[0]
@@ -140,7 +147,7 @@
         scale = active / (real * real + imag2)
         g_ref[0, k] = real * scale
         g_ref[1, k] = -imag * scale
-    write_toeplitz(shifts_ref, emission_ref, absorption_ref, mix_ref)
+    write_toeplitz(shifts_ref, emission_ref, absorption_ref, mix_ref, *send_ref.shape[:2])
 
     total = kweight_ref[0]
     for k in range(1, kweight_ref.shape[0]):
@@ -235,16 +242,13 @@
 
 
 def mix_kernel(got_ref, mix_ref, less_ref, great_ref):
-    count = mix_ref.shape[0]
-    got = got_ref[...].astype(F32)
-    dens = jnp.sum(got, axis=1).reshape(count, got.shape[3])
+    depth = mix_ref.shape[0]
+    count = mix_ref.shape[1] // 4
+    dens = got_ref[...].astype(F32).reshape(depth, got_ref.shape[3]).astype(BF16)
     out = lax.dot_general(
-        dens,
-        mix_ref[...],
-        (((0,), (0,)), ((), ())),
-        precision=lax.Precision.HIGHEST,
-        preferred_element_type=F32,
-    )
+        dens, mix_ref[...], (((0,), (0,)), ((), ())), preferred_element_type=F32
+    )
+    out = out[:, : 2 * count] + out[:, 2 * count :]
     block = less_ref.shape[1]
     less_ref[0] = out[:block, :count]
     great_ref[0] = out[block:, count:]
@@ -290,7 +294,7 @@
         basis,
     )
     send_shape = jax.ShapeDtypeStruct((energy_devs, k_devs, ecount, 2 * block), BF16)
-    mix_shape = jax.ShapeDtypeStruct((all_energies, 2 * all_energies), F32)
+    mix_shape = jax.ShapeDtypeStruct((k_devs * all_energies, 4 * all_energies), BF16)
     scratch = (
         [SMEM(a.shape, a.dtype) for a in operands[1:3]]
         + [VMEM(a.shape, a.dtype) for a in operands[3:11]]

time: 20.2 us -> 20.1 us (level)
  no operation moved by 1% of the time
where the time goes in v3:
time: 20.1 us; the launch traced here: 19.9 us
  blocking collectives  14.7 us (73%)
  Pallas kernels  3.92 us (20%)
  between operations  1.29 us (6%)
    all_to_all x1, blocking collectives, on_device(): lax.all_to_all(send.reshape(energy_devs * k_devs, ecount, 2 * block), ('e...  14.7 us
    pallas_call x1, Pallas kernels, layer(): pl.pallas_call(functools.partial(layer_kernel, has_prev), out_shape=(send...  3.09 us
    pallas_call x1, Pallas kernels, on_device(): pl.pallas_call(mix_kernel, out_shape=(out_shape, out_shape), in_specs=[vm...  0.83 us

profile of v3, /device:TPU:0, one launch (start us, length us, event | category | flops | bytes accessed | tf_op | source)
XLA Modules:
  0.0 19.9 jit_solution(16353459691137406670)
XLA Ops:
  1.3 3.1 %shard_map.131 = (bf16[16,2,8,128]{3,2,1,0:T(8,128)(2,1)S(1)}, bf16[256,512]{1,0:T(8,128)(2,1)S(1)}) custom-call(s32[1]{0:T(128)S(6)} %copy.14.count_ref, f32[4]{0:T(128)} %trans_hbm.1, s32[8]{0:T(128)} %kweight_hbm.1, s32[1,512]{1,0:T(1,128)} %bitcast.8, f32[1,512]{1,0:T(1,128)} %bitcast.9, f32[1,512]{1,0:T(1,128)} %bitcast.10, f32[1,1024]{1,0:T(1,128)} %levels_hbm.1, ...), custom_call_target="tpu_custom_call" | custom-call | tf_op jit(solution)/shard_map/pallas_call | solution.py:316
  4.4 14.7 %all_to_all.5 = bf16[32,8,128]{2,1,0:T(8,128)(2,1)S(1)} all-to-all(bf16[32,8,128]{2,1,0:T(8,128)(2,1)S(1)} %bitcast.7), channel_id=1, replica_groups=mesh['layer'=1,'energy'=16,'kpt'=2] {'energy','kpt'}, dimensions={0} | all-to-all | bytes 131072 | tf_op jit(solution)/shard_map/all_to_all | solution.py:339
  19.1 0.8 %shard_map.132 = (f32[1,64,128]{2,1,0:T(8,128)}, f32[1,64,128]{2,1,0:T(8,128)}) custom-call(bf16[16,2,8,128]{3,2,1,0:T(8,128)(2,1)S(1)} %bitcast.6, bf16[256,512]{1,0:T(8,128)(2,1)S(1)} %get-tuple-element.5.mix_ref), custom_call_target="tpu_custom_call" | custom-call | tf_op jit(solution)/shard_map/pallas_call | solution.py:343

commit v4 on v3

--- a/solution.py
+++ b/solution.py
@@ -54,9 +54,9 @@
         skewed = pltpu.roll(square, 0, 1, stride=1, stride_axis=0)[:, :count]
         high = skewed.astype(BF16).astype(F32)
         for side, piece in enumerate((high, skewed - high)):
-            blocks = piece.reshape(energy_devs, 1, count // energy_devs, count)
+            blocks = piece[None]
             blocks = jnp.broadcast_to(
-                blocks, (energy_devs, k_devs, count // energy_devs, count)
+                blocks, (k_devs, count, count)
             ).reshape(k_devs * count, count)
             first = (2 * side + which) * count
             mix_ref[:, first : first + count] = blocks.astype(BF16)
@@ -147,7 +147,7 @@
         scale = active / (real * real + imag2)
         g_ref[0, k] = real * scale
         g_ref[1, k] = -imag * scale
-    write_toeplitz(shifts_ref, emission_ref, absorption_ref, mix_ref, *send_ref.shape[:2])
+    write_toeplitz(shifts_ref, emission_ref, absorption_ref, mix_ref, *send_ref.shape[1::-1])
 
     total = kweight_ref[0]
     for k in range(1, kweight_ref.shape[0]):
@@ -183,8 +183,8 @@
             group = pl.ds(rows + k * ecount * modes, ecount * modes)
             z_ref[group, cols] = jnp.concatenate(z_im, axis=0).astype(BF16)
 
-    copies_k = send_ref.shape[1]
-    block = width // send_ref.shape[0]
+    copies_k = send_ref.shape[0]
+    block = width // send_ref.shape[1]
 
     def densities(part, psi):
         if has_prev:
@@ -206,7 +206,7 @@
                 [less[:, t * block : (t + 1) * block], great[:, t * block : (t + 1) * block]], axis=1
             ).astype(BF16)
             for c in range(copies_k):
-                send_ref[part * (chunk // block) + t, c] = both
+                send_ref[c, part * (chunk // block) + t] = both
 
     wide[0].wait()
     x_ref[...] = src_ref[0].reshape(2 * rows, width)
@@ -293,7 +293,7 @@
         source,
         basis,
     )
-    send_shape = jax.ShapeDtypeStruct((energy_devs, k_devs, ecount, 2 * block), BF16)
+    send_shape = jax.ShapeDtypeStruct((k_devs, energy_devs, ecount, 2 * block), BF16)
     mix_shape = jax.ShapeDtypeStruct((k_devs * all_energies, 4 * all_energies), BF16)
     scratch = (
         [SMEM(a.shape, a.dtype) for a in operands[1:3]]
@@ -337,8 +337,8 @@
         stored = tuple(jnp.zeros(a.shape, a.dtype) for a in (send_shape, mix_shape, psi_shape))
         send, mix, _ = lax.fori_loop(0, layer_devs, sweep, (stored[2], stored))[1]
     got = lax.all_to_all(
-        send.reshape(energy_devs * k_devs, ecount, 2 * block), ("energy", "kpt"), 0, 0, tiled=True
-    ).reshape(energy_devs, k_devs, ecount, 2 * block)
+        send.reshape(energy_devs * k_devs, ecount, 2 * block), ("kpt", "energy"), 0, 0, tiled=True
+    ).reshape(k_devs, energy_devs, ecount, 2 * block)
     out_shape = jax.ShapeDtypeStruct((1, block, all_energies), F32)
     return pl.pallas_call(
         mix_kernel,

time: 20.1 us -> 19.9 us (0.990)
  no operation moved by 1% of the time
where the time goes in v4:
time: 19.9 us; the launch traced here: 19.7 us
  blocking collectives  14.5 us (73%)
  Pallas kernels  3.92 us (20%)
  between operations  1.29 us (6%)
    all_to_all x1, blocking collectives, on_device(): lax.all_to_all(send.reshape(energy_devs * k_devs, ecount, 2 * block), ('k...  14.5 us
    pallas_call x1, Pallas kernels, layer(): pl.pallas_call(functools.partial(layer_kernel, has_prev), out_shape=(send...  3.09 us
    pallas_call x1, Pallas kernels, on_device(): pl.pallas_call(mix_kernel, out_shape=(out_shape, out_shape), in_specs=[vm...  0.83 us

profile of v4, /device:TPU:0, one launch (start us, length us, event | category | flops | bytes accessed | tf_op | source)
XLA Modules:
  0.0 19.7 jit_solution(5183210219807952012)
XLA Ops:
  1.3 3.1 %shard_map.131 = (bf16[2,16,8,128]{3,2,1,0:T(8,128)(2,1)S(1)}, bf16[256,512]{1,0:T(8,128)(2,1)S(1)}) custom-call(s32[1]{0:T(128)S(6)} %copy.14.count_ref, f32[4]{0:T(128)} %trans_hbm.1, s32[8]{0:T(128)} %kweight_hbm.1, s32[1,512]{1,0:T(1,128)} %bitcast.8, f32[1,512]{1,0:T(1,128)} %bitcast.9, f32[1,512]{1,0:T(1,128)} %bitcast.10, f32[1,1024]{1,0:T(1,128)} %levels_hbm.1, ...), custom_call_target="tpu_custom_call" | custom-call | tf_op jit(solution)/shard_map/pallas_call | solution.py:316
  4.4 14.5 %all_to_all.5 = bf16[32,8,128]{2,1,0:T(8,128)(2,1)S(1)} all-to-all(bf16[32,8,128]{2,1,0:T(8,128)(2,1)S(1)} %bitcast.7), channel_id=1, replica_groups=mesh['layer'=1,'energy'=16,'kpt'=2] {'kpt','energy'}, dimensions={0} | all-to-all | bytes 131072 | tf_op jit(solution)/shard_map/all_to_all | solution.py:339
  18.9 0.8 %shard_map.132 = (f32[1,64,128]{2,1,0:T(8,128)}, f32[1,64,128]{2,1,0:T(8,128)}) custom-call(bf16[2,16,8,128]{3,2,1,0:T(8,128)(2,1)S(1)} %bitcast.6, bf16[256,512]{1,0:T(8,128)(2,1)S(1)} %get-tuple-element.5.mix_ref), custom_call_target="tpu_custom_call" | custom-call | tf_op jit(solution)/shard_map/pallas_call | solution.py:343

commit v5 on v4

--- a/solution.py
+++ b/solution.py
@@ -21,7 +21,7 @@
 
 
 def chunk_of(width):
-    return 256 if width % 256 == 0 else width
+    return 512 if width % 512 == 0 else width
 
 
 def in_three(value):

time: 19.9 us -> 19.9 us (level)
  no operation moved by 1% of the time
where the time goes in v5:
time: 19.9 us; the launch traced here: 19.7 us
  blocking collectives  14.5 us (73%)
  Pallas kernels  3.93 us (20%)
  between operations  1.29 us (6%)
    all_to_all x1, blocking collectives, on_device(): lax.all_to_all(send.reshape(energy_devs * k_devs, ecount, 2 * block), ('k...  14.5 us
    pallas_call x1, Pallas kernels, layer(): pl.pallas_call(functools.partial(layer_kernel, has_prev), out_shape=(send...  3.1 us
    pallas_call x1, Pallas kernels, on_device(): pl.pallas_call(mix_kernel, out_shape=(out_shape, out_shape), in_specs=[vm...  0.83 us

profile of v5, /device:TPU:0, one launch (start us, length us, event | category | flops | bytes accessed | tf_op | source)
XLA Modules:
  0.0 19.7 jit_solution(5919698446349457580)
XLA Ops:
  1.3 3.1 %shard_map.131 = (bf16[2,16,8,128]{3,2,1,0:T(8,128)(2,1)S(1)}, bf16[256,512]{1,0:T(8,128)(2,1)S(1)}) custom-call(s32[1]{0:T(128)S(6)} %copy.14.count_ref, f32[4]{0:T(128)} %trans_hbm.1, s32[8]{0:T(128)} %kweight_hbm.1, s32[1,512]{1,0:T(1,128)} %bitcast.8, f32[1,512]{1,0:T(1,128)} %bitcast.9, f32[1,512]{1,0:T(1,128)} %bitcast.10, f32[1,1024]{1,0:T(1,128)} %levels_hbm.1, ...), custom_call_target="tpu_custom_call" | custom-call | tf_op jit(solution)/shard_map/pallas_call | solution.py:316
  4.4 14.5 %all_to_all.5 = bf16[32,8,128]{2,1,0:T(8,128)(2,1)S(1)} all-to-all(bf16[32,8,128]{2,1,0:T(8,128)(2,1)S(1)} %bitcast.7), channel_id=1, replica_groups=mesh['layer'=1,'energy'=16,'kpt'=2] {'kpt','energy'}, dimensions={0} | all-to-all | bytes 131072 | tf_op jit(solution)/shard_map/all_to_all | solution.py:339
  18.9 0.8 %shard_map.132 = (f32[1,64,128]{2,1,0:T(8,128)}, f32[1,64,128]{2,1,0:T(8,128)}) custom-call(bf16[2,16,8,128]{3,2,1,0:T(8,128)(2,1)S(1)} %bitcast.6, bf16[256,512]{1,0:T(8,128)(2,1)S(1)} %get-tuple-element.5.mix_ref), custom_call_target="tpu_custom_call" | custom-call | tf_op jit(solution)/shard_map/pallas_call | solution.py:343
